TPU v7x, 32 devices: a whole 2x2x4 slice. The times are simulated.
32 devices in a mesh: grp: 2 (over y), col: 4 (over z), row: 4 (over x, core).
Axes of the slice: x: 2, y: 2, z: 4, core: 2. Of those that a mesh axis runs over, the one named last changes fastest.
Arguments:
- spectra: bfloat16 [2, 8, 256, 2048], P(None, None, ('grp', 'col'), 'row'), parts along dimension 2, may hold values from -6 to 6
- pair_mask: int32 [8, 4], P('grp', 'col'), parts along dimension 0, may hold values from 0 to 1, as said below
Outputs:
- correlations: bfloat16 [32, 4, 256, 1024], P('row', None, ('grp', 'col')), parts along dimension 2
There are 2 independent parts, one for each index of `grp`. A program takes and returns all parts, laid end to end along the dimension named above; each array names one. Nothing has to cross between parts.
Inputs may be any that keep to these rules, and one draw needn't show every extreme that they name: pair_mask[k, b] is 0 wherever b + k >= 4.
All inputs are finite; a program needn't handle non-finite values.
Results may differ from a plain program's by a relative error of at most 0.0033.
Values may be sent and summed in bfloat16 or wider, within the bound.
A program may use at most 128 MiB of HBM per device.

v0:
```python
import functools
import math

import jax
import jax.numpy as jnp
import numpy as np
from jax import lax
from jax.experimental import pallas as pl
from jax.experimental.pallas import tpu as pltpu
from jax.sharding import PartitionSpec as P

WIN = 8
F = 2048
L = 1024
NFFT = 65536
LO_BIN = 2048
GROUP = 8
ROWS = WIN * GROUP
LANES = 128
MESH = pl.DeviceIdType.MESH


def lag_tables(shards):
    bins = LO_BIN + np.arange(F, dtype=np.int32)
    lags = np.arange(L, dtype=np.int32) - L // 2
    turns = np.mod(bins[:, None] * lags[None, :], NFFT).astype(np.float32)
    phase = (turns * np.float32(2.0 * math.pi / NFFT)).astype(np.float64)
    parts = [
        part.astype(np.float32).astype(jnp.bfloat16).reshape(shards, F // shards, L)
        for part in (np.cos(phase), -np.sin(phase))
    ]
    return np.concatenate(parts, axis=1)


def xor(index, mask):
    result = index
    bit = 1
    while bit <= mask:
        if mask & bit:
            result = result + bit - 2 * bit * lax.rem(lax.div(index, bit), 2)
        bit *= 2
    return result


def schedule(shards, offsets):
    far = range(2, shards)
    events = [("T", 0, 1), ("X", 0, 0), ("T", 0, 2), ("O", 1), ("X", 0, 1)]
    events += [("T", 0, m) for m in far if m > 2]
    events += [("T", 1, 0), ("X", 1, 0), ("T", 1, 1), ("X", 1, 1)]
    events += [("T", 1, m) for m in far]
    events += [("T", 2, 0), ("X", 2, 0), ("O", 2), ("O", 3), ("X", 0, 2), ("T", 2, 1), ("X", 0, 3)]
    events += [("X", 1, 2), ("T", 2, 2), ("X", 1, 3), ("T", 2, 3), ("X", 2, 1), ("T", 3, 0), ("X", 2, 2)]
    events += [("X", 2, 3), ("T", 3, 1), ("X", 3, 0), ("T", 3, 2), ("X", 3, 1), ("X", 3, 2)]
    events += [("T", 3, 3), ("X", 3, 3)]
    for m in range(4, shards):
        events += [("O", m), ("T", 2, m), ("T", 3, m)]
        events += [("X", k, m) for k in range(offsets)]
    return events


def kernel(
    shards, blocks, offsets, spectra, mask, table_hbm, out,
    owner, partner, table, products, total, sums,
    table_sem, o_send, o_recv, t_send, t_recv, z_send, z_recv,
):
    me = lax.axis_index("row")
    block = lax.axis_index("col")
    bins = spectra.shape[3]
    groups = owner.shape[1]
    mine = groups * GROUP // shards
    left = lax.rem(block + blocks - 1, blocks)
    right = lax.rem(block + 1, blocks)

    load = pltpu.make_async_copy(table_hbm, table, table_sem)
    load.start()

    barrier = pltpu.get_barrier_semaphore()
    for m in range(1, shards):
        pl.semaphore_signal(barrier, inc=1, device_id={"row": xor(me, m)}, device_id_type=MESH)

    @pl.when(block > 0)
    def _():
        pl.semaphore_signal(barrier, inc=1, device_id={"col": left}, device_id_type=MESH)

    @pl.when(block < blocks - 1)
    def _():
        pl.semaphore_signal(barrier, inc=1, device_id={"col": right}, device_id_type=MESH)

    def whiten(step, carry):
        lanes = pl.ds(pl.multiple_of(step * LANES, LANES), LANES)
        for pair in range(WIN // 2):
            parts = []
            for w in (2 * pair, 2 * pair + 1):
                re = spectra[0, w, :, lanes].astype(jnp.float32)
                im = spectra[1, w, :, lanes].astype(jnp.float32)
                denom = jnp.maximum(jnp.sqrt(re * re + im * im), 0.5)
                parts.append((re / denom, im / denom))
            for c in range(2):
                for g in range(groups):
                    rows = slice(g * GROUP, (g + 1) * GROUP)
                    both = jnp.concatenate([parts[0][c][rows], parts[1][c][rows]], axis=0)
                    owner[0, g, pl.ds(c * ROWS + pair * 2 * GROUP, 2 * GROUP), lanes] = both.astype(jnp.bfloat16)
        return carry

    lax.fori_loop(0, bins // LANES, whiten, 0)

    def group_of(row):
        return lax.div(row * mine, GROUP)

    partner[0, 0] = owner[0, group_of(me)]

    inner = (block > 0).astype(jnp.int32) + (block < blocks - 1).astype(jnp.int32)
    pl.semaphore_wait(barrier, inner + (shards - 1))

    def z_copy(k, m):
        return pltpu.make_async_remote_copy(
            src_ref=partner.at[k - 1, m], dst_ref=partner.at[k, m],
            send_sem=z_send.at[k - 1, m], recv_sem=z_recv.at[k - 1, m],
            device_id={"col": left}, device_id_type=MESH,
        )

    def t_copy(m):
        peer = xor(me, m)
        return pltpu.make_async_remote_copy(
            src_ref=owner.at[0, group_of(peer)], dst_ref=partner.at[0, m],
            send_sem=t_send.at[m], recv_sem=t_recv.at[m],
            device_id={"row": peer}, device_id_type=MESH,
        )

    def o_copy(m):
        relayed = m % 2 == 1 and m > 1
        return pltpu.make_async_remote_copy(
            src_ref=owner.at[m - 1 if relayed else 0], dst_ref=owner.at[m],
            send_sem=o_send.at[m], recv_sem=o_recv.at[m],
            device_id={"row": xor(me, 1 if relayed else m)}, device_id_type=MESH,
        )

    def forward(k, m):
        if k < offsets:
            @pl.when((block > 0) & (block + k - 1 < blocks))
            def _():
                z_copy(k, m).start()

    forward(1, 0)
    for m in range(1, shards):
        t_copy(m).start()
    o_copy(1).start()
    for m in range(2, shards, 2):
        o_copy(m).start()
    load.wait()

    first_row = lax.rem(me * mine, GROUP) if mine < GROUP else 0

    def correlate(k, m):
        chunk = xor(me, m)
        re = partner[k, m, :ROWS, :].astype(jnp.float32)
        im = partner[k, m, ROWS:, :].astype(jnp.float32)
        for number, rows in enumerate((re, re + im, im - re)):
            kept = rows
            for offset in range(mine, GROUP, mine):
                moved = jnp.concatenate([rows[offset:], rows[:offset]], axis=0)
                kept = jnp.where(first_row == offset, moved, kept)
            sums[number] = kept
        steps = bins // LANES

        def tile(step, carry):
            g = lax.div(step, steps)
            at = pl.multiple_of(lax.rem(step, steps) * LANES, LANES)
            lanes = pl.ds(at, LANES)
            a = owner[m, g, :ROWS, lanes].astype(jnp.float32)
            b = owner[m, g, ROWS:, lanes].astype(jnp.float32)
            a = [a[w * GROUP:(w + 1) * GROUP] for w in range(WIN)]
            b = [b[w * GROUP:(w + 1) * GROUP] for w in range(WIN)]
            p = [x - y for x, y in zip(a, b)]
            for pair in range(mine // 2):
                reals, imags = [], []
                for j in (2 * pair, 2 * pair + 1):
                    s = [None, None, None]
                    for w in range(WIN):
                        row = pl.ds(w * GROUP + j, 1)
                        terms = (
                            p[w] * sums[0, row, lanes],
                            b[w] * sums[1, row, lanes],
                            a[w] * sums[2, row, lanes],
                        )
                        s = [t if x is None else x + t for x, t in zip(s, terms)]
                    reals.append(s[0] + s[1])
                    imags.append(s[0] + s[2])
                rows = pl.ds(pl.multiple_of(g * (mine * GROUP) + pair * 2 * GROUP, 2 * GROUP), 2 * GROUP)
                products[rows, lanes] = jnp.concatenate(reals, axis=0).astype(jnp.bfloat16)
                products[rows, pl.ds(at + bins, LANES)] = jnp.concatenate(imags, axis=0).astype(jnp.bfloat16)
            return carry

        lax.fori_loop(0, groups * steps, tile, 0)
        wide = 256

        def lags(step, carry):
            columns = pl.ds(pl.multiple_of(step * wide, wide), wide)
            part = jnp.dot(products[...], table[chunk, :, columns], preferred_element_type=jnp.float32)
            if m > 0:
                part = part + total[k, :, columns]
            total[k, :, columns] = part
            return carry

        lax.fori_loop(0, L // wide, lags, 0)

    def finish(k):
        factor = mask[k, 0].astype(jnp.float32) * (1.0 / math.sqrt(F * WIN))
        for j in range(mine):
            for g in range(0, groups, 2):
                pieces = [total[k, pl.ds(((g + s) * mine + j) * GROUP, GROUP), :] for s in range(2)]
                both = jnp.concatenate(pieces, axis=0) * factor
                out[j, k, pl.ds(g * GROUP, 2 * GROUP), :] = both.astype(out.dtype)

    done = [0] * offsets
    for event in schedule(shards, offsets):
        if event[0] == "O":
            m = event[1]
            o_copy(m).wait_recv()
            if m % 2 == 0:
                o_copy(m + 1).start()
        elif event[0] == "T":
            k, m = event[1:]
            if k == 0:
                t_copy(m).wait_recv()
            else:
                @pl.when(block + k < blocks)
                def _(k=k, m=m):
                    z_copy(k, m).wait_recv()
            forward(k + 1, m)
        else:
            k, m = event[1:]
            done[k] += 1

            @pl.when(block + k < blocks)
            def _(k=k, m=m):
                correlate(k, m)
                if done[k] == shards:
                    finish(k)

            if done[k] == shards and k > 0:
                @pl.when(block + k >= blocks)
                def _(k=k):
                    out[:, k] = jnp.zeros((mine, groups * GROUP, L), out.dtype)

    for m in range(1, shards):
        t_copy(m).wait_send()
        o_copy(m).wait_send()
    for k in range(1, offsets):
        @pl.when((block > 0) & (block + k - 1 < blocks))
        def _(k=k):
            for m in range(shards):
                z_copy(k, m).wait_send()


def body(shards, blocks, spectra, pair_mask):
    channels, bins = spectra.shape[2:]
    offsets = pair_mask.shape[0]
    groups = channels // GROUP
    mine = channels // shards
    table = lag_tables(shards)
    chunk = (2 * ROWS, bins)
    pairs = mine * channels
    dma = pltpu.SemaphoreType.DMA
    return pl.pallas_call(
        functools.partial(kernel, shards, blocks, offsets),
        out_shape=jax.ShapeDtypeStruct((mine, offsets, channels, L), jnp.bfloat16),
        in_specs=[
            pl.BlockSpec(memory_space=pltpu.VMEM),
            pl.BlockSpec(memory_space=pltpu.SMEM),
            pl.BlockSpec(memory_space=pl.ANY),
        ],
        out_specs=pl.BlockSpec(memory_space=pltpu.VMEM),
        scratch_shapes=[
            pltpu.VMEM((shards, groups) + chunk, jnp.bfloat16),
            pltpu.VMEM((offsets, shards) + chunk, jnp.bfloat16),
            pltpu.VMEM(table.shape, jnp.bfloat16),
            pltpu.VMEM((pairs, 2 * bins), jnp.bfloat16),
            pltpu.VMEM((offsets, pairs, L), jnp.float32),
            pltpu.VMEM((3, ROWS, bins), jnp.float32),
            dma,
            dma((shards,)),
            dma((shards,)),
            dma((shards,)),
            dma((shards,)),
            dma((offsets - 1, shards)),
            dma((offsets - 1, shards)),
        ],
        compiler_params=pltpu.CompilerParams(
            collective_id=0, has_side_effects=True, vmem_limit_bytes=48 * 1024 * 1024
        ),
    )(spectra, pair_mask, table)


def solution(mesh):
    return jax.shard_map(
        functools.partial(body, mesh.shape["row"], mesh.shape["col"]),
        mesh=mesh,
        in_specs=(P(None, None, ("grp", "col"), "row"), P("grp", "col")),
        out_specs=P("row", None, ("grp", "col"), None),
        check_vma=False,
    )
```

profile of v0, /device:TPU:0, one launch (start us, length us, event | category | flops | bytes accessed | tf_op | source)
XLA Modules:
  0.0 55.6 jit_solution(4740621416226984434)
XLA Ops:
  0.0 0.7 %copy.4.mask = s32[4,1]{1,0:T(4,128)S(1)} copy(s32[4,1]{0,1:T(1,128)} %param.4) | data formatting | bytes 32 | tf_op args[1]
  0.7 0.0 copy-start
  0.7 1.0 %copy-done = bf16[2,8,32,512]{3,2,1,0:T(8,128)(2,1)S(1)} copy-done((bf16[2,8,32,512]{3,2,1,0:T(8,128)(2,1)S(1)}, bf16[2,8,32,512]{3,2,1,0:T(8,128)(2,1)}, u32[]{:S(2)}) %copy-start) | copy-done | bytes 524312
  1.8 52.5 %shard_map.37 = bf16[8,4,32,1024]{3,2,1,0:T(8,128)(2,1)S(1)} custom-call(bf16[2,8,32,512]{3,2,1,0:T(8,128)(2,1)S(1)} %copy-done, s32[4,1]{1,0:T(4,128)S(1)} %copy.4.mask, bf16[4,1024,1024]{2,1,0:T(8,128)(2,1)} %constant.2.clone.table_hbm), custom_call_target="tpu_custom_call" | custom-call | tf_op jit(solution)/shard_map/pallas_call | solution.py:265
  54.3 1.3 %copy.6 = bf16[8,4,32,1024]{3,2,1,0:T(8,128)(2,1)} copy(bf16[8,4,32,1024]{3,2,1,0:T(8,128)(2,1)S(1)} %shard_map.37) | data formatting | bytes 4194304
Async XLA Ops:
  0.7 1.0 %copy-start = (bf16[2,8,32,512]{3,2,1,0:T(8,128)(2,1)S(1)}, bf16[2,8,32,512]{3,2,1,0:T(8,128)(2,1)}, u32[]{:S(2)}) copy-start(bf16[2,8,32,512]{3,2,1,0:T(8,128)(2,1)} %spectra.1) | copy-start | bytes 1572868
where the time goes:
time: 56.3 us; the launch traced here: 55.6 us
  Pallas kernels  52.5 us (93%)
  local copies, waits for them, and re-layouts  3.1 us (6%)
    pallas_call x1, Pallas kernels, body(): pl.pallas_call(functools.partial(kernel, shards, blocks, offsets), out_sh...  52.5 us
    unnamed x4, local copies, waits for them, and re-layouts  3.1 us

commit v1 on v0

--- a/solution.py
+++ b/solution.py
@@ -59,9 +59,9 @@
 
 
 def kernel(
-    shards, blocks, offsets, spectra, mask, table_hbm, out,
-    owner, partner, table, products, total, sums,
-    table_sem, o_send, o_recv, t_send, t_recv, z_send, z_recv,
+    shards, blocks, offsets, spectra_hbm, mask, table_hbm, out,
+    spectra, owner, partner, table, products, total, sums,
+    spectra_sem, table_sem, o_send, o_recv, t_send, t_recv, z_send, z_recv,
 ):
     me = lax.axis_index("row")
     block = lax.axis_index("col")
@@ -72,7 +72,8 @@
     right = lax.rem(block + 1, blocks)
 
     load = pltpu.make_async_copy(table_hbm, table, table_sem)
-    load.start()
+    fetch = pltpu.make_async_copy(spectra_hbm, spectra, spectra_sem)
+    fetch.start()
 
     barrier = pltpu.get_barrier_semaphore()
     for m in range(1, shards):
@@ -102,6 +103,8 @@
                     owner[0, g, pl.ds(c * ROWS + pair * 2 * GROUP, 2 * GROUP), lanes] = both.astype(jnp.bfloat16)
         return carry
 
+    fetch.wait()
+    load.start()
     lax.fori_loop(0, bins // LANES, whiten, 0)
 
     def group_of(row):
@@ -151,8 +154,10 @@
 
     first_row = lax.rem(me * mine, GROUP) if mine < GROUP else 0
 
-    def correlate(k, m):
-        chunk = xor(me, m)
+    steps = bins // LANES
+    wide = L // groups
+
+    def prepare(k, m):
         re = partner[k, m, :ROWS, :].astype(jnp.float32)
         im = partner[k, m, ROWS:, :].astype(jnp.float32)
         for number, rows in enumerate((re, re + im, im - re)):
@@ -161,58 +166,72 @@
                 moved = jnp.concatenate([rows[offset:], rows[:offset]], axis=0)
                 kept = jnp.where(first_row == offset, moved, kept)
             sums[number] = kept
-        steps = bins // LANES
-
-        def tile(step, carry):
-            g = lax.div(step, steps)
-            at = pl.multiple_of(lax.rem(step, steps) * LANES, LANES)
-            lanes = pl.ds(at, LANES)
-            a = owner[m, g, :ROWS, lanes].astype(jnp.float32)
-            b = owner[m, g, ROWS:, lanes].astype(jnp.float32)
-            a = [a[w * GROUP:(w + 1) * GROUP] for w in range(WIN)]
-            b = [b[w * GROUP:(w + 1) * GROUP] for w in range(WIN)]
-            p = [x - y for x, y in zip(a, b)]
-            for pair in range(mine // 2):
-                reals, imags = [], []
-                for j in (2 * pair, 2 * pair + 1):
-                    s = [None, None, None]
-                    for w in range(WIN):
-                        row = pl.ds(w * GROUP + j, 1)
-                        terms = (
-                            p[w] * sums[0, row, lanes],
-                            b[w] * sums[1, row, lanes],
-                            a[w] * sums[2, row, lanes],
-                        )
-                        s = [t if x is None else x + t for x, t in zip(s, terms)]
-                    reals.append(s[0] + s[1])
-                    imags.append(s[0] + s[2])
-                rows = pl.ds(pl.multiple_of(g * (mine * GROUP) + pair * 2 * GROUP, 2 * GROUP), 2 * GROUP)
-                products[rows, lanes] = jnp.concatenate(reals, axis=0).astype(jnp.bfloat16)
-                products[rows, pl.ds(at + bins, LANES)] = jnp.concatenate(imags, axis=0).astype(jnp.bfloat16)
+
+    def cross(m, slot, g, step):
+        lanes = pl.ds(step * LANES, LANES)
+        a = owner[m, g, :ROWS, lanes].astype(jnp.float32)
+        b = owner[m, g, ROWS:, lanes].astype(jnp.float32)
+        a = [a[w * GROUP:(w + 1) * GROUP] for w in range(WIN)]
+        b = [b[w * GROUP:(w + 1) * GROUP] for w in range(WIN)]
+        p = [x - y for x, y in zip(a, b)]
+        for pair in range(mine // 2):
+            reals, imags = [], []
+            for j in (2 * pair, 2 * pair + 1):
+                s = [None, None, None]
+                for w in range(WIN):
+                    row = pl.ds(w * GROUP + j, 1)
+                    terms = (
+                        p[w] * sums[0, row, lanes],
+                        b[w] * sums[1, row, lanes],
+                        a[w] * sums[2, row, lanes],
+                    )
+                    s = [t if x is None else x + t for x, t in zip(s, terms)]
+                reals.append(s[0] + s[1])
+                imags.append(s[0] + s[2])
+            rows = pl.ds(pl.multiple_of(g * (mine * GROUP) + pair * 2 * GROUP, 2 * GROUP), 2 * GROUP)
+            products[slot, rows, lanes] = jnp.concatenate(reals, axis=0).astype(jnp.bfloat16)
+            products[slot, rows, pl.ds(bins + step * LANES, LANES)] = jnp.concatenate(imags, axis=0).astype(jnp.bfloat16)
+
+    def lags(k, m, slot, g):
+        columns = pl.ds(pl.multiple_of(g * wide, wide), wide)
+        part = jnp.dot(products[slot], table[xor(me, m), :, columns], preferred_element_type=jnp.float32)
+        if m > 0:
+            part = part + total[k, :, columns]
+        total[k, :, columns] = part
+
+    def work(task, earlier):
+        if task:
+            prepare(*task[:2])
+
+        def one(g, carry):
+            if earlier:
+                lags(*earlier, g)
+            if task:
+                for step in range(steps):
+                    cross(task[1], task[2], g, step)
             return carry
 
-        lax.fori_loop(0, groups * steps, tile, 0)
-        wide = 256
-
-        def lags(step, carry):
-            columns = pl.ds(pl.multiple_of(step * wide, wide), wide)
-            part = jnp.dot(products[...], table[chunk, :, columns], preferred_element_type=jnp.float32)
-            if m > 0:
-                part = part + total[k, :, columns]
-            total[k, :, columns] = part
-            return carry
-
-        lax.fori_loop(0, L // wide, lags, 0)
+        lax.fori_loop(0, groups, one, 0)
+        if earlier and earlier[1] == shards - 1:
+            finish(earlier[0])
 
     def finish(k):
-        factor = mask[k, 0].astype(jnp.float32) * (1.0 / math.sqrt(F * WIN))
+        factor = mask[0, k].astype(jnp.float32) * (1.0 / math.sqrt(F * WIN))
         for j in range(mine):
             for g in range(0, groups, 2):
                 pieces = [total[k, pl.ds(((g + s) * mine + j) * GROUP, GROUP), :] for s in range(2)]
                 both = jnp.concatenate(pieces, axis=0) * factor
                 out[j, k, pl.ds(g * GROUP, 2 * GROUP), :] = both.astype(out.dtype)
 
-    done = [0] * offsets
+    def active(k):
+        return block + k < blocks
+
+    for k in range(1, offsets):
+        @pl.when(block + k >= blocks)
+        def _(k=k):
+            out[:, k] = jnp.zeros((mine, groups * GROUP, L), out.dtype)
+
+    pending, slot = None, 0
     for event in schedule(shards, offsets):
         if event[0] == "O":
             m = event[1]
@@ -229,19 +248,29 @@
                     z_copy(k, m).wait_recv()
             forward(k + 1, m)
         else:
-            k, m = event[1:]
-            done[k] += 1
-
-            @pl.when(block + k < blocks)
-            def _(k=k, m=m):
-                correlate(k, m)
-                if done[k] == shards:
-                    finish(k)
-
-            if done[k] == shards and k > 0:
-                @pl.when(block + k >= blocks)
-                def _(k=k):
-                    out[:, k] = jnp.zeros((mine, groups * GROUP, L), out.dtype)
+            task = event[1:] + (slot,)
+            k = task[0]
+            older = pending[0] if pending else k
+
+            @pl.when(active(max(k, older)))
+            def _(task=task, pending=pending):
+                work(task, pending)
+
+            if older < k:
+                @pl.when(active(older) & (block + k >= blocks))
+                def _(pending=pending):
+                    work(None, pending)
+
+            if older > k:
+                @pl.when(active(k) & (block + older >= blocks))
+                def _(task=task):
+                    work(task, None)
+
+            pending, slot = task, 1 - slot
+
+    @pl.when(active(pending[0]))
+    def _():
+        work(None, pending)
 
     for m in range(1, shards):
         t_copy(m).wait_send()
@@ -266,18 +295,20 @@
         functools.partial(kernel, shards, blocks, offsets),
         out_shape=jax.ShapeDtypeStruct((mine, offsets, channels, L), jnp.bfloat16),
         in_specs=[
-            pl.BlockSpec(memory_space=pltpu.VMEM),
+            pl.BlockSpec(memory_space=pl.ANY),
             pl.BlockSpec(memory_space=pltpu.SMEM),
             pl.BlockSpec(memory_space=pl.ANY),
         ],
         out_specs=pl.BlockSpec(memory_space=pltpu.VMEM),
         scratch_shapes=[
+            pltpu.VMEM(spectra.shape, jnp.bfloat16),
             pltpu.VMEM((shards, groups) + chunk, jnp.bfloat16),
             pltpu.VMEM((offsets, shards) + chunk, jnp.bfloat16),
             pltpu.VMEM(table.shape, jnp.bfloat16),
-            pltpu.VMEM((pairs, 2 * bins), jnp.bfloat16),
+            pltpu.VMEM((2, pairs, 2 * bins), jnp.bfloat16),
             pltpu.VMEM((offsets, pairs, L), jnp.float32),
             pltpu.VMEM((3, ROWS, bins), jnp.float32),
+            dma,
             dma,
             dma((shards,)),
             dma((shards,)),
@@ -289,7 +320,7 @@
         compiler_params=pltpu.CompilerParams(
             collective_id=0, has_side_effects=True, vmem_limit_bytes=48 * 1024 * 1024
         ),
-    )(spectra, pair_mask, table)
+    )(spectra, pair_mask.T, table)
 
 
 def solution(mesh):

time: 56.3 us -> 52.5 us (0.933)
  Pallas kernels: 52.5 us -> 49.3 us
    pallas_call x1, Pallas kernels: 52.5 us -> 49.3 us  [body(): pl.pallas_call(functools.partial(kernel, shards, blocks, offsets), out_sh...]
    unnamed x4 -> x5, local copies, waits for them, and re-layouts: 3.1 us -> 3.02 us
where the time goes in v1:
time: 52.5 us; the launch traced here: 52.3 us
  Pallas kernels  49.3 us (94%)
  local copies, waits for them, and re-layouts  3.02 us (6%)
    pallas_call x1, Pallas kernels, body(): pl.pallas_call(functools.partial(kernel, shards, blocks, offsets), out_sh...  49.3 us
    unnamed x5, local copies, waits for them, and re-layouts  3.02 us

profile of v1, /device:TPU:0, one launch (start us, length us, event | category | flops | bytes accessed | tf_op | source)
XLA Modules:
  0.0 52.3 jit_solution(17758255149166151415)
XLA Ops:
  0.0 0.0 copy-start
  0.0 1.0 %copy-done = bf16[2,8,32,512]{3,2,1,0:T(8,128)(2,1)S(1)} copy-done((bf16[2,8,32,512]{3,2,1,0:T(8,128)(2,1)S(1)}, bf16[2,8,32,512]{3,2,1,0:T(8,128)(2,1)}, u32[]{:S(2)}) %copy-start) | copy-done | bytes 524312
  1.0 0.0 copy-start.1
  1.0 0.7 %copy-done.1 = s32[4,1]{0,1:T(1,128)S(1)} copy-done((s32[4,1]{0,1:T(1,128)S(1)}, s32[4,1]{0,1:T(1,128)}, u32[]{:S(2)}) %copy-start.1) | copy-done | bytes 40
  1.7 49.3 %shard_map.37 = bf16[8,4,32,1024]{3,2,1,0:T(8,128)(2,1)S(1)} custom-call(bf16[2,8,32,512]{3,2,1,0:T(8,128)(2,1)S(1)} %copy-done, s32[1,4]{1,0:T(1,128)S(1)} %bitcast.1, bf16[4,1024,1024]{2,1,0:T(8,128)(2,1)} %constant.2.clone.table_hbm), custom_call_target="tpu_custom_call" | custom-call | tf_op jit(solution)/shard_map/pallas_call | solution.py:294
  51.0 1.3 %copy.5 = bf16[8,4,32,1024]{3,2,1,0:T(8,128)(2,1)} copy(bf16[8,4,32,1024]{3,2,1,0:T(8,128)(2,1)S(1)} %shard_map.37) | data formatting | bytes 4194304
Async XLA Ops:
  0.0 1.0 %copy-start = (bf16[2,8,32,512]{3,2,1,0:T(8,128)(2,1)S(1)}, bf16[2,8,32,512]{3,2,1,0:T(8,128)(2,1)}, u32[]{:S(2)}) copy-start(bf16[2,8,32,512]{3,2,1,0:T(8,128)(2,1)} %spectra_hbm.1) | copy-start | bytes 1572868
  1.0 0.7 %copy-start.1 = (s32[4,1]{0,1:T(1,128)S(1)}, s32[4,1]{0,1:T(1,128)}, u32[]{:S(2)}) copy-start(s32[4,1]{0,1:T(1,128)} %param.4) | copy-start | bytes 52

commit v2 on v1

--- a/solution.py
+++ b/solution.py
@@ -48,8 +48,8 @@
     events += [("T", 0, m) for m in far if m > 2]
     events += [("T", 1, 0), ("X", 1, 0), ("T", 1, 1), ("X", 1, 1)]
     events += [("T", 1, m) for m in far]
-    events += [("T", 2, 0), ("X", 2, 0), ("O", 2), ("O", 3), ("X", 0, 2), ("T", 2, 1), ("X", 0, 3)]
-    events += [("X", 1, 2), ("T", 2, 2), ("X", 1, 3), ("T", 2, 3), ("X", 2, 1), ("T", 3, 0), ("X", 2, 2)]
+    events += [("T", 2, 0), ("X", 2, 0), ("T", 2, 1), ("O", 2), ("X", 2, 1), ("O", 3), ("X", 0, 2)]
+    events += [("T", 2, 2), ("X", 0, 3), ("X", 1, 2), ("T", 2, 3), ("X", 1, 3), ("T", 3, 0), ("X", 2, 2)]
     events += [("X", 2, 3), ("T", 3, 1), ("X", 3, 0), ("T", 3, 2), ("X", 3, 1), ("X", 3, 2)]
     events += [("T", 3, 3), ("X", 3, 3)]
     for m in range(4, shards):

time: 52.5 us -> 51.4 us (0.979)
  Pallas kernels: 49.3 us -> 48.2 us
    pallas_call x1, Pallas kernels: 49.3 us -> 48.2 us  [body(): pl.pallas_call(functools.partial(kernel, shards, blocks, offsets), out_sh...]
where the time goes in v2:
time: 51.4 us; the launch traced here: 51.2 us
  Pallas kernels  48.2 us (94%)
  local copies, waits for them, and re-layouts  3.02 us (6%)
    pallas_call x1, Pallas kernels, body(): pl.pallas_call(functools.partial(kernel, shards, blocks, offsets), out_sh...  48.2 us
    unnamed x5, local copies, waits for them, and re-layouts  3.02 us

profile of v2, /device:TPU:0, one launch (start us, length us, event | category | flops | bytes accessed | tf_op | source)
XLA Modules:
  0.0 51.2 jit_solution(15028022050742319517)
XLA Ops:
  0.0 0.0 copy-start
  0.0 1.0 %copy-done = bf16[2,8,32,512]{3,2,1,0:T(8,128)(2,1)S(1)} copy-done((bf16[2,8,32,512]{3,2,1,0:T(8,128)(2,1)S(1)}, bf16[2,8,32,512]{3,2,1,0:T(8,128)(2,1)}, u32[]{:S(2)}) %copy-start) | copy-done | bytes 524312
  1.0 0.0 copy-start.1
  1.0 0.7 %copy-done.1 = s32[4,1]{0,1:T(1,128)S(1)} copy-done((s32[4,1]{0,1:T(1,128)S(1)}, s32[4,1]{0,1:T(1,128)}, u32[]{:S(2)}) %copy-start.1) | copy-done | bytes 40
  1.7 48.2 %shard_map.37 = bf16[8,4,32,1024]{3,2,1,0:T(8,128)(2,1)S(1)} custom-call(bf16[2,8,32,512]{3,2,1,0:T(8,128)(2,1)S(1)} %copy-done, s32[1,4]{1,0:T(1,128)S(1)} %bitcast.1, bf16[4,1024,1024]{2,1,0:T(8,128)(2,1)} %constant.2.clone.table_hbm), custom_call_target="tpu_custom_call" | custom-call | tf_op jit(solution)/shard_map/pallas_call | solution.py:294
  49.9 1.3 %copy.5 = bf16[8,4,32,1024]{3,2,1,0:T(8,128)(2,1)} copy(bf16[8,4,32,1024]{3,2,1,0:T(8,128)(2,1)S(1)} %shard_map.37) | data formatting | bytes 4194304
Async XLA Ops:
  0.0 1.0 %copy-start = (bf16[2,8,32,512]{3,2,1,0:T(8,128)(2,1)S(1)}, bf16[2,8,32,512]{3,2,1,0:T(8,128)(2,1)}, u32[]{:S(2)}) copy-start(bf16[2,8,32,512]{3,2,1,0:T(8,128)(2,1)} %spectra_hbm.1) | copy-start | bytes 1572868
  1.0 0.7 %copy-start.1 = (s32[4,1]{0,1:T(1,128)S(1)}, s32[4,1]{0,1:T(1,128)}, u32[]{:S(2)}) copy-start(s32[4,1]{0,1:T(1,128)} %param.4) | copy-start | bytes 52
